TPU v7x, 512 devices: a whole 4x4x16 slice. The times are simulated.
512 devices in a mesh: gx: 32 (over z_hi, x, core), gy: 16 (over y, z_lo).
Axes of the slice: x: 4, y: 4, z: 16 (z_hi: 4, z_lo: 4; z = z_hi * 4 + z_lo), core: 2. Of those that a mesh axis runs over, the one named last changes fastest.
Arguments:
- feats: bfloat16 [32, 16, 2, 128, 512], P('gx', 'gy'), may hold values from -12 to 12
- w_query: bfloat16 [512, 512], replicated, may hold values from -1 to 1
- w_key: bfloat16 [512, 512], replicated, may hold values from -1 to 1
- w_value: bfloat16 [512, 512], replicated, may hold values from -0.25 to 0.25
- out_grad: bfloat16 [32, 16, 2, 128, 512], P('gx', 'gy'), may hold values from -6 to 6
- patch_count: int32 [32, 16], P('gx', 'gy'), may hold values from 1 to 2
- point_count: int32 [32, 16, 2], P('gx', 'gy'), may hold values from 32 to 128
- neighbours: int32 [32, 16, 2, 3], P('gx', 'gy'), may hold values from 0 to 9, as said below
- neighbour_points: int32 [32, 16, 2, 3], P('gx', 'gy'), may hold values from 32 to 128, as said below
Outputs:
- mixed: bfloat16 [32, 16, 2, 128, 512], P('gx', 'gy')
- feat_grad: bfloat16 [32, 16, 2, 128, 512], P('gx', 'gy')
- grad_query: bfloat16 [512, 512], replicated
- grad_key: bfloat16 [512, 512], replicated
- grad_value: bfloat16 [512, 512], replicated
Inputs may be any that keep to these rules, and one draw needn't show every extreme that they name: `neighbour_points`: equal to point_count of the patch that the same entry of neighbours names.
All inputs are finite; a program needn't handle non-finite values.
Results may differ from a plain program's by a relative error of at most 0.015.
Values may be sent and summed in bfloat16 or wider, within the bound.
A program may use at most 64 MiB of HBM per device.

v0:
```python
import jax
import jax.numpy as jnp
from jax import lax
from jax.sharding import PartitionSpec as P

HEADS = 8


def with_halo(x, sides, width):
    for axis, dim in sides:
        peers, length = (lax.axis_size(axis), x.shape[dim])
        up = [(i, (i + 1) % peers) for i in range(peers - 1)]
        down = [(j, i) for i, j in up]
        last = lax.slice_in_dim(x, length - width, length, axis=dim)
        initial = lax.slice_in_dim(x, 0, width, axis=dim)
        before = lax.ppermute(last, axis, up)
        after = lax.ppermute(initial, axis, down)
        x = jnp.concatenate([before, x, after], axis=dim)
    return x


def passed_along(value, axis, steps):
    count = lax.axis_size(axis)
    initial, last = (max(0, -steps), min(count, count - steps))
    return lax.ppermute(value, axis, [(source, source + steps) for source in range(initial, last)])


def one_slot(items):
    qq, keys, key_valid, live, grads = items
    points, width = qq.shape
    head_dim = width // HEADS
    scale = head_dim ** (-0.5)
    kk = keys[:, :width].reshape(-1, HEADS, head_dim)
    vv = keys[:, width:].reshape(-1, HEADS, head_dim)
    qh = qq.reshape(points, HEADS, head_dim)
    scores = jnp.einsum("qhd,khd->hqk", qh, kk, preferred_element_type=jnp.float32) * scale
    scores = jnp.where(key_valid[None, None, :], scores, -1e30)
    top = jnp.max(scores, axis=-1, keepdims=True)
    expo = jnp.exp(scores - top)
    probs = expo / jnp.sum(expo, axis=-1, keepdims=True)
    probs_b = probs.astype(jnp.bfloat16)
    mixed = jnp.einsum("hqk,khd->qhd", probs_b, vv, preferred_element_type=jnp.float32)
    alive = live[:, None, None]
    out = jnp.where(alive, mixed, 0.0).astype(jnp.bfloat16).reshape(points, width)
    gradh = grads.reshape(points, HEADS, head_dim)
    dout = jnp.where(alive, gradh, jnp.zeros_like(gradh))
    dprob = jnp.einsum("qhd,khd->hqk", dout, vv, preferred_element_type=jnp.float32)
    inner = jnp.sum(probs * dprob, axis=-1, keepdims=True)
    dscore = (probs * (dprob - inner) * scale).astype(jnp.bfloat16)
    dquery = jnp.einsum("hqk,khd->qhd", dscore, kk, preferred_element_type=jnp.float32)
    dquery = dquery.astype(jnp.bfloat16).reshape(points, width)
    dkey = jnp.einsum("hqk,qhd->khd", dscore, qh, preferred_element_type=jnp.float32)
    dval = jnp.einsum("hqk,qhd->khd", probs_b, dout, preferred_element_type=jnp.float32)
    contrib = jnp.concatenate(
        [dkey.reshape(-1, points, width), dval.reshape(-1, points, width)], axis=-1
    )
    return (out, dquery, contrib)


def attend(query, table, codes, key_len, q_valid, grad_out):
    slots, points, width = query.shape
    keys = table.reshape(-1, points, 2 * width)[codes].reshape(slots, -1, 2 * width)
    key_valid = (jnp.arange(points, dtype=jnp.int32)[None, None, :] < key_len[:, :, None]).reshape(
        slots, -1
    )
    out, dquery, contrib = lax.map(one_slot, (query, keys, key_valid, q_valid, grad_out))
    contrib = contrib.reshape(-1, points * 2 * width)
    onehot = (jnp.arange(5 * slots, dtype=jnp.int32)[:, None] == codes.reshape(1, -1)).astype(
        jnp.float32
    )
    partial_value = jnp.dot(
        onehot, contrib, precision=lax.Precision.HIGHEST, preferred_element_type=jnp.float32
    )
    partial_value = partial_value.astype(jnp.bfloat16).reshape(5, slots, points, 2 * width)
    return (out, dquery, partial_value)


def faces_of(wide):
    return jnp.stack([wide[0, 1], wide[2, 1], wide[1, 0], wide[1, 2]])


def project(rows, weight):
    return jnp.dot(rows, weight, preferred_element_type=jnp.float32).astype(jnp.bfloat16)


def body(
    feats, w_query, w_key, w_value, out_grad, patch_count, point_count, neighbours, neighbour_points
):
    slots, points, width = (feats.shape[2], feats.shape[3], feats.shape[4])
    flat = feats.reshape(-1, width)
    query = project(flat, w_query).reshape(slots, points, width)
    keyval = jnp.concatenate([project(flat, w_key), project(flat, w_value)], axis=-1).reshape(
        slots, points, 2 * width
    )
    wide = with_halo(keyval[None, None], (("gx", 0), ("gy", 1)), 1)
    faces = faces_of(wide)
    table = jnp.concatenate([keyval[None], faces], axis=0)
    codes = jnp.concatenate([jnp.arange(slots, dtype=jnp.int32)[:, None], neighbours[0, 0]], axis=1)
    counts = point_count[0, 0]
    key_len = jnp.concatenate([counts[:, None], neighbour_points[0, 0]], axis=1)
    q_valid = (jnp.arange(slots, dtype=jnp.int32)[:, None] < patch_count[0, 0]) & (
        jnp.arange(points, dtype=jnp.int32)[None, :] < counts[:, None]
    )
    out, dquery, partial_value = attend(query, table, codes, key_len, q_valid, out_grad[0, 0])
    total = partial_value[0].astype(jnp.float32)
    for shift_by, place in ((-1, 1), (1, 2)):
        total = total + passed_along(partial_value[place], "gx", shift_by).astype(jnp.float32)
    for shift_by, place in ((-1, 3), (1, 4)):
        total = total + passed_along(partial_value[place], "gy", shift_by).astype(jnp.float32)
    grads = total.astype(jnp.bfloat16)
    dq = dquery.reshape(-1, width)
    dk = grads[..., :width].reshape(-1, width)
    dv = grads[..., width:].reshape(-1, width)
    back = (((1,), (1,)), ((), ()))
    feat_grad = (
        lax.dot_general(dq, w_query, back, preferred_element_type=jnp.float32)
        + lax.dot_general(dk, w_key, back, preferred_element_type=jnp.float32)
        + lax.dot_general(dv, w_value, back, preferred_element_type=jnp.float32)
    )
    feat_grad = feat_grad.astype(jnp.bfloat16).reshape(feats.shape)
    outer = (((0,), (0,)), ((), ()))
    local_q = lax.dot_general(flat, dq, outer, preferred_element_type=jnp.float32)
    local_k = lax.dot_general(flat, dk, outer, preferred_element_type=jnp.float32)
    local_v = lax.dot_general(flat, dv, outer, preferred_element_type=jnp.float32)
    sum_q, sum_k, sum_v = lax.psum((local_q, local_k, local_v), ("gx", "gy"))
    mixed = out.reshape(feats.shape)
    return (
        mixed,
        feat_grad,
        sum_q.astype(jnp.bfloat16),
        sum_k.astype(jnp.bfloat16),
        sum_v.astype(jnp.bfloat16),
    )


def solution(mesh):
    return jax.shard_map(
        body,
        mesh=mesh,
        in_specs=(
            P("gx", "gy", None, None, None),
            P(),
            P(),
            P(),
            P("gx", "gy", None, None, None),
            P("gx", "gy"),
            P("gx", "gy", None),
            P("gx", "gy", None, None),
            P("gx", "gy", None, None),
        ),
        out_specs=(P("gx", "gy", None, None, None), P("gx", "gy", None, None, None), P(), P(), P()),
        check_vma=False,
    )
```

profile of v0, /device:TPU:8, one launch (start us, length us, event | category | flops | bytes accessed | tf_op | source)
XLA Modules:
  0.0 444.8 jit_solution(17124175754200817036)
XLA Ops:
  5.0 3.1 collective-permute-start
  10.9 3.8 collective-permute-start.2
  15.7 4.7 %collective-permute-start.3 = (bf16[3,1,2,128,1024]{4,3,2,1,0:T(8,128)(2,1)}, bf16[3,1,2,128,1024]{4,3,2,1,0:T(8,128)(2,1)S(1)}, u32[]{:S(2)}, u32[]{:S(2)}) collective-permute-start(bf16[3,1,2,128,1024]{4,3,2,1,0:T(8,128)(2,1)} %pad_maximum_fusion), channel_id=1, source_target_pairs={{1,0},{2,1},{3,2},{4,3},{5,4},{6,5},{7,6},{8,7},{9,8},{10,9},{11,1... | collective-permute-start | bytes 4718600 | tf_op jit(solution)/shard_map/ppermute | solution.py:17
  24.1 39.3 %collective-permute-done.2 = bf16[3,1,2,128,1024]{4,3,2,1,0:T(8,128)(2,1)} collective-permute-done((bf16[3,1,2,128,1024]{4,3,2,1,0:T(8,128)(2,1)}, bf16[3,1,2,128,1024]{4,3,2,1,0:T(8,128)(2,1)}, u32[]{:S(2)}, u32[]{:S(2)}) %collective-permute-start.2) | collective-permute-done | bytes 1572896 | tf_op jit(solution)/shard_map/ppermute | solution.py:16
  63.4 1.9 fusion.46
  65.3 22.7 %collective-permute-done.3 = bf16[3,1,2,128,1024]{4,3,2,1,0:T(8,128)(2,1)S(1)} collective-permute-done((bf16[3,1,2,128,1024]{4,3,2,1,0:T(8,128)(2,1)}, bf16[3,1,2,128,1024]{4,3,2,1,0:T(8,128)(2,1)S(1)}, u32[]{:S(2)}, u32[]{:S(2)}) %collective-permute-start.3) | collective-permute-done | bytes 1572896 | tf_op jit(solution)/shard_map/ppermute | solution.py:17
  88.8 3.8 gather_fusion
  92.6 81.0 %while.14 = (s32[]{:T(128)}, bf16[2,128,512]{2,1,0:T(8,128)(2,1)}, bf16[2,128,512]{2,1,0:T(8,128)(2,1)}, f32[2,4,128,1024]{3,2,1,0:T(8,128)}, pred[2,128]{1,0:T(...) while((s32[]{:T(128)}, bf16[2,128,512]{2,1,0:T(8,128)(2,1)}, ...), condition=%wide.region_4.5_spmd, body=%wide.region_0.4_spmd.sunk | while | flops 415043072 | bytes 50373096 | solution.py:66
  99.0 3.9 fusion.108
  102.9 2.8 fusion.110
  105.7 8.5 %fusion.109 = bf16[8,64,128]{2,1,0:T(8,128)(2,1)} fusion(bf16[512,8,64]{0,2,1:T(8,128)(2,1)} %bitcast.165, f32[8,128,512]{2,1,0:T(8,128)S(1)} %fusion.107, f32[8,128,512]{2,1,0:T(8,128)} %get-tuple-element.182, f32[8,128]{1,0:T(8,128)S(1)} %copy-done.16), kind=kOutput, calls=%fused_computation.15.clone.1 | convolution fusion | flops 70845952 | bytes 4853760 | tf_op jit(solution)/shard_map/while/body/eval_jaxpr/hqk,khd->qhd/dot_general | solution.py:50
  114.2 8.8 %fusion.111 = f32[512,8,64]{0,2,1:T(8,128)} fusion(bf16[128,8,64]{0,2,1:T(8,128)(2,1)S(1)} %bitcast.180, f32[8,128,512]{2,1,0:T(8,128)S(1)} %fusion.107, f32[8,128,512]{2,1,0:T(8,128)} %get-tuple-element.182, f32[8,128]{1,0:T(8,128)S(1)} %copy-done.16), kind=kOutput, calls=%fused_computation.12.clone.1 | convolution fusion | flops 70780416 | bytes 5378048 | tf_op jit(solution)/shard_map/while/body/eval_jaxpr/hqk,qhd->khd/dot_general | solution.py:52
  123.0 2.0 convolution_bitcast_fusion.5
  128.7 2.0 copy.65
  139.5 3.9 fusion.108
  143.4 2.8 fusion.110
  146.2 8.5 %fusion.109 = bf16[8,64,128]{2,1,0:T(8,128)(2,1)} fusion(bf16[512,8,64]{0,2,1:T(8,128)(2,1)} %bitcast.165, f32[8,128,512]{2,1,0:T(8,128)S(1)} %fusion.107, f32[8,128,512]{2,1,0:T(8,128)} %get-tuple-element.182, f32[8,128]{1,0:T(8,128)S(1)} %copy-done.16), kind=kOutput, calls=%fused_computation.15.clone.1 | convolution fusion | flops 70845952 | bytes 4853760 | tf_op jit(solution)/shard_map/while/body/eval_jaxpr/hqk,khd->qhd/dot_general | solution.py:50
  154.7 8.8 %fusion.111 = f32[512,8,64]{0,2,1:T(8,128)} fusion(bf16[128,8,64]{0,2,1:T(8,128)(2,1)S(1)} %bitcast.180, f32[8,128,512]{2,1,0:T(8,128)S(1)} %fusion.107, f32[8,128,512]{2,1,0:T(8,128)} %get-tuple-element.182, f32[8,128]{1,0:T(8,128)S(1)} %copy-done.16), kind=kOutput, calls=%fused_computation.12.clone.1 | convolution fusion | flops 70780416 | bytes 5378048 | tf_op jit(solution)/shard_map/while/body/eval_jaxpr/hqk,qhd->khd/dot_general | solution.py:52
  163.5 2.0 convolution_bitcast_fusion.5
  167.4 1.8 maximum_bitcast_fusion.2
  169.2 2.0 copy.65
  173.6 4.6 %copy.40 = f32[1,8,128,1024]{3,1,2,0:T(8,128)S(1)} copy(f32[1,8,128,1024]{3,2,1,0:T(8,128)} %bitcast.176) | data formatting | bytes 8388608
  178.3 3.6 convolution_convert_fusion
  181.9 1.9 fusion.50
  184.2 4.7 %collective-permute-start.5 = (bf16[2,128,1024]{2,1,0:T(8,128)(2,1)S(1)}, bf16[2,128,1024]{2,1,0:T(8,128)(2,1)S(1)}, u32[]{:S(2)}, u32[]{:S(2)}) collective-permute-start(bf16[2,128,1024]{2,1,0:T(8,128)(2,1)S(1)} %bitcast.195), channel_id=1, source_target_pairs={{0,16},{16,32},{32,48},{48,64},{64,80},{80,96},{96,112},{112,128},... | collective-permute-start | bytes 1572872 | tf_op jit(solution)/shard_map/ppermute | solution.py:25
  188.9 10.2 %collective-permute-start.6 = (bf16[2,128,1024]{2,1,0:T(8,128)(2,1)S(1)}, bf16[2,128,1024]{2,1,0:T(8,128)(2,1)S(1)}, u32[]{:S(2)}, u32[]{:S(2)}) collective-permute-start(bf16[2,128,1024]{2,1,0:T(8,128)(2,1)S(1)} %bitcast.194), channel_id=1, source_target_pairs={{1,0},{2,1},{3,2},{4,3},{5,4},{6,5},{7,6},{8,7},{9,8},{10,9},{11,1... | collective-permute-start | bytes 1572872 | tf_op jit(solution)/shard_map/ppermute | solution.py:25
  199.1 1.9 collective-permute-start.7
  203.1 8.4 %collective-permute-done.6 = bf16[2,128,1024]{2,1,0:T(8,128)(2,1)S(1)} collective-permute-done((bf16[2,128,1024]{2,1,0:T(8,128)(2,1)S(1)}, bf16[2,128,1024]{2,1,0:T(8,128)(2,1)S(1)}, u32[]{:S(2)}, u32[]{:S(2)}) %collective-permute-start.6) | collective-permute-done | bytes 524320 | tf_op jit(solution)/shard_map/ppermute | solution.py:25
  211.5 18.7 %collective-permute-done.7 = bf16[2,128,1024]{2,1,0:T(8,128)(2,1)S(1)} collective-permute-done((bf16[2,128,1024]{2,1,0:T(8,128)(2,1)S(1)}, bf16[2,128,1024]{2,1,0:T(8,128)(2,1)S(1)}, u32[]{:S(2)}, u32[]{:S(2)}) %collective-permute-start.7) | collective-permute-done | bytes 524320 | tf_op jit(solution)/shard_map/ppermute | solution.py:25
  234.6 205.1 %all-reduce.2 = (bf16[512,512]{0,1:T(8,128)(2,1)}, bf16[512,512]{0,1:T(8,128)(2,1)}, bf16[512,512]{0,1:T(8,128)(2,1)S(1)}) all-reduce(f32[512,512]{0,1:T(8,128)S(1)} %convolution_bitcast_fusion.3, f32[512,512]{0,1:T(8,128)S(1)} %convolution_bitcast_fusion.2, ...), channel_id=1, replica_groups=mesh['gx'=32,'gy'=16] {'gx','gy'}, use_global_device_ids=true, to_apply=%region_5.6 | all-reduce | flops 786432 | bytes 4718592 | tf_op jit(solution)/shard_map/psum | solution.py:125
  439.7 2.0 copy.28
  441.8 2.0 copy.29
  (127 shorter events, 42.8 us)
Async XLA Ops:
  0.6 20.7 %copy-start = (bf16[512,512]{1,0:T(8,128)(2,1)S(1)}, bf16[512,512]{1,0:T(8,128)(2,1)}, u32[]{:S(2)}) copy-start(bf16[512,512]{1,0:T(8,128)(2,1)} %param.12) | copy-start | bytes 1572868
  0.6 8.0 %copy-start.13 = (s32[1,1,2]{2,1,0:T(1,128)S(1)}, s32[1,1,2]{2,1,0:T(1,128)}, u32[]{:S(2)}) copy-start(s32[1,1,2]{2,1,0:T(1,128)} %param.17) | copy-start | bytes 28
  0.7 8.1 %copy-start.11 = (s32[1,1,2,3]{3,2,1,0:T(2,128)S(1)}, s32[1,1,2,3]{3,2,1,0:T(2,128)}, u32[]{:S(2)}) copy-start(s32[1,1,2,3]{3,2,1,0:T(2,128)} %param.18) | copy-start | bytes 76
  0.7 8.3 %copy-start.12 = (s32[1,1,2,3]{3,2,1,0:T(2,128)S(1)}, s32[1,1,2,3]{3,2,1,0:T(2,128)}, u32[]{:S(2)}) copy-start(s32[1,1,2,3]{3,2,1,0:T(2,128)} %param.19) | copy-start | bytes 76
  3.6 11.2 %copy-start.10 = (bf16[1,1,2,128,512]{4,3,2,1,0:T(8,128)(2,1)S(1)}, bf16[1,1,2,128,512]{4,3,2,1,0:T(8,128)(2,1)}, u32[]{:S(2)}) copy-start(bf16[1,1,2,128,512]{4,3,2,1,0:T(8,128)(2,1)} %param.15) | copy-start | bytes 786436
  3.7 5.5 %collective-permute-start.1 = (bf16[1,1,2,128,1024]{4,3,2,1,0:T(8,128)(2,1)S(1)}, bf16[1,1,2,128,1024]{4,3,2,1,0:T(8,128)(2,1)S(1)}, u32[]{:S(2)}, u32[]{:S(2)}) collective-permute-start(bf16[1,1,2,128,1024]{4,3,2,1,0:T(8,128)(2,1)S(1)} %bitcast.172), channel_id=1, source_target_pairs={{16,0},{32,16},{48,32},{64,48},{80,64},{96,80},{112,96},{128,112},... | collective-permute-start | bytes 1572872 | tf_op jit(solution)/shard_map/ppermute | solution.py:17
  5.0 4.6 %collective-permute-start = (bf16[1,1,2,128,1024]{4,3,2,1,0:T(8,128)(2,1)S(1)}, bf16[1,1,2,128,1024]{4,3,2,1,0:T(8,128)(2,1)S(1)}, u32[]{:S(2)}, u32[]{:S(2)}) collective-permute-start(bf16[1,1,2,128,1024]{4,3,2,1,0:T(8,128)(2,1)S(1)} %bitcast.173), channel_id=1, source_target_pairs={{0,16},{16,32},{32,48},{48,64},{64,80},{80,96},{96,112},{112,128},... | collective-permute-start | bytes 1572872 | tf_op jit(solution)/shard_map/ppermute | solution.py:16
  9.1 12.3 %copy-start.1 = (bf16[1,1,2,128,512]{4,3,2,1,0:T(8,128)(2,1)S(1)}, bf16[1,1,2,128,512]{4,3,2,1,0:T(8,128)(2,1)}, u32[]{:S(2)}) copy-start(bf16[1,1,2,128,512]{4,3,2,1,0:T(8,128)(2,1)} %param.11) | copy-start | bytes 786436
  10.9 52.5 %collective-permute-start.2 = (bf16[3,1,2,128,1024]{4,3,2,1,0:T(8,128)(2,1)}, bf16[3,1,2,128,1024]{4,3,2,1,0:T(8,128)(2,1)}, u32[]{:S(2)}, u32[]{:S(2)}) collective-permute-start(bf16[3,1,2,128,1024]{4,3,2,1,0:T(8,128)(2,1)} %pad_maximum_fusion), channel_id=1, source_target_pairs={{0,1},{1,2},{2,3},{3,4},{4,5},{5,6},{6,7},{7,8},{8,9},{9,10},{10,1... | collective-permute-start | bytes 4718600 | tf_op jit(solution)/shard_map/ppermute | solution.py:16
  15.7 72.2 %collective-permute-start.3 = (bf16[3,1,2,128,1024]{4,3,2,1,0:T(8,128)(2,1)}, bf16[3,1,2,128,1024]{4,3,2,1,0:T(8,128)(2,1)S(1)}, u32[]{:S(2)}, u32[]{:S(2)}) collective-permute-start(bf16[3,1,2,128,1024]{4,3,2,1,0:T(8,128)(2,1)} %pad_maximum_fusion), channel_id=1, source_target_pairs={{1,0},{2,1},{3,2},{4,3},{5,4},{6,5},{7,6},{8,7},{9,8},{10,9},{11,1... | collective-permute-start | bytes 4718600 | tf_op jit(solution)/shard_map/ppermute | solution.py:17
  102.9 2.8 copy-start.16
  105.7 8.5 %copy-start.3 = (bf16[1,128,512]{1,2,0:T(8,128)(2,1)S(1)}, bf16[1,128,512]{1,2,0:T(8,128)(2,1)}, u32[]{:S(2)}) copy-start(bf16[1,128,512]{1,2,0:T(8,128)(2,1)} %copy.62) | copy-start | bytes 393220 | tf_op jit(solution)/shard_map/while
  128.7 2.0 copy-start.4
  128.7 2.1 copy-start.2
  128.7 2.3 copy-start.7
  131.7 1.5 copy-start.8
  131.7 1.5 copy-start.15
  133.1 0.5 copy-start.14
  143.4 2.8 copy-start.16
  146.2 8.5 %copy-start.3 = (bf16[1,128,512]{1,2,0:T(8,128)(2,1)S(1)}, bf16[1,128,512]{1,2,0:T(8,128)(2,1)}, u32[]{:S(2)}) copy-start(bf16[1,128,512]{1,2,0:T(8,128)(2,1)} %copy.62) | copy-start | bytes 393220 | tf_op jit(solution)/shard_map/while
  169.2 2.0 copy-start.4
  169.2 2.1 copy-start.2
  169.2 2.3 copy-start.7
  172.2 1.5 copy-start.8
  172.2 1.5 copy-start.15
  183.7 18.6 %copy-start.9 = (bf16[2,128,512]{2,1,0:T(8,128)(2,1)S(1)}, bf16[2,128,512]{2,1,0:T(8,128)(2,1)}, u32[]{:S(2)}) copy-start(bf16[2,128,512]{2,1,0:T(8,128)(2,1)} %get-tuple-element.55) | copy-start | bytes 786436
  184.2 18.8 %collective-permute-start.5 = (bf16[2,128,1024]{2,1,0:T(8,128)(2,1)S(1)}, bf16[2,128,1024]{2,1,0:T(8,128)(2,1)S(1)}, u32[]{:S(2)}, u32[]{:S(2)}) collective-permute-start(bf16[2,128,1024]{2,1,0:T(8,128)(2,1)S(1)} %bitcast.195), channel_id=1, source_target_pairs={{0,16},{16,32},{32,48},{48,64},{64,80},{80,96},{96,112},{112,128},... | collective-permute-start | bytes 1572872 | tf_op jit(solution)/shard_map/ppermute | solution.py:25
  188.9 22.5 %collective-permute-start.6 = (bf16[2,128,1024]{2,1,0:T(8,128)(2,1)S(1)}, bf16[2,128,1024]{2,1,0:T(8,128)(2,1)S(1)}, u32[]{:S(2)}, u32[]{:S(2)}) collective-permute-start(bf16[2,128,1024]{2,1,0:T(8,128)(2,1)S(1)} %bitcast.194), channel_id=1, source_target_pairs={{1,0},{2,1},{3,2},{4,3},{5,4},{6,5},{7,6},{8,7},{9,8},{10,9},{11,1... | collective-permute-start | bytes 1572872 | tf_op jit(solution)/shard_map/ppermute | solution.py:25
  199.1 31.1 %collective-permute-start.7 = (bf16[2,128,1024]{2,1,0:T(8,128)(2,1)S(1)}, bf16[2,128,1024]{2,1,0:T(8,128)(2,1)S(1)}, u32[]{:S(2)}, u32[]{:S(2)}) collective-permute-start(bf16[2,128,1024]{2,1,0:T(8,128)(2,1)S(1)} %bitcast.193), channel_id=1, source_target_pairs={{0,1},{1,2},{2,3},{3,4},{4,5},{5,6},{6,7},{7,8},{8,9},{9,10},{10,1... | collective-permute-start | bytes 1572872 | tf_op jit(solution)/shard_map/ppermute | solution.py:25
  201.1 29.1 %collective-permute-start.4 = (bf16[2,128,1024]{2,1,0:T(8,128)(2,1)S(1)}, bf16[2,128,1024]{2,1,0:T(8,128)(2,1)S(1)}, u32[]{:S(2)}, u32[]{:S(2)}) collective-permute-start(bf16[2,128,1024]{2,1,0:T(8,128)(2,1)S(1)} %bitcast.192), channel_id=1, source_target_pairs={{16,0},{32,16},{48,32},{64,48},{80,64},{96,80},{112,96},{128,112},... | collective-permute-start | bytes 1572872 | tf_op jit(solution)/shard_map/ppermute | solution.py:25
  230.9 1.0 copy-start.5
  231.9 1.6 copy-start.6
  (1 other events, 0.5 us)
where the time goes:
time: 446 us; the launch traced here: 445 us
  blocking collectives  205 us (46%)
  waiting for transfers between devices  89.5 us (20%)
  matrix products  64.1 us (14%)
  local copies, waits for them, and re-layouts  45.5 us (10%)
  starting transfers between devices  31 us (7%)
  other arithmetic  7.84 us (2%)
    psum x1, blocking collectives, body(): sum_q, sum_k, sum_v = lax.psum((local_q, local_k, local_v), ('gx', 'gy'))  205 us
    ppermute x2, waiting for transfers between devices, with_halo(): before = lax.ppermute(last, axis, up)  39.7 us
    ppermute x4, waiting for transfers between devices, passed_along(): lax.ppermute(value, axis, [(source, source + steps) for source in range(i...  27.2 us
    ppermute x2, waiting for transfers between devices, with_halo(): after = lax.ppermute(initial, axis, down)  22.7 us
    ppermute x4, starting transfers between devices, passed_along(): lax.ppermute(value, axis, [(source, source + steps) for source in range(i...  18.1 us
    dot_general x2, matrix products, one_slot(): jnp.einsum('hqk,qhd->khd', dscore, qh, preferred_element_type=jnp.float32)  17.6 us
    dot_general x2, matrix products, one_slot(): jnp.einsum('hqk,khd->qhd', dscore, kk, preferred_element_type=jnp.float32)  17.1 us
    unnamed x32, local copies, waits for them, and re-layouts  16.2 us
  transfers between devices with their start and end apart: 8, of which 5 were waited for; matrix products, arithmetic and copies ran while one was open for 2% of the time, Pallas kernels for 0%

commit v1 on v0

--- a/solution.py
+++ b/solution.py
@@ -122,7 +122,7 @@
     local_q = lax.dot_general(flat, dq, outer, preferred_element_type=jnp.float32)
     local_k = lax.dot_general(flat, dk, outer, preferred_element_type=jnp.float32)
     local_v = lax.dot_general(flat, dv, outer, preferred_element_type=jnp.float32)
-    sum_q, sum_k, sum_v = lax.psum((local_q, local_k, local_v), ("gx", "gy"))
+    sum_q, sum_k, sum_v = lax.psum(lax.psum((local_q, local_k, local_v), "gy"), "gx")
     mixed = out.reshape(feats.shape)
     return (
         mixed,

time: 446 us -> 690 us (1.55)
  the two profiles are of different devices: /device:TPU:8 before, /device:TPU:104 now
where the time goes in v1:
time: 690 us; the launch traced here: 689 us
  waiting for transfers between devices  303 us (44%)
  blocking collectives  229 us (33%)
  matrix products  66.2 us (10%)
  local copies, waits for them, and re-layouts  43.4 us (6%)
  starting transfers between devices  24.5 us (4%)
  between operations  15 us (2%)
  other arithmetic  7.87 us (1%)
    psum x1, blocking collectives, body(): lax.psum(lax.psum((local_q, local_k, local_v), 'gy'), 'gx')  229 us
    psum x1, waiting for transfers between devices, body(): lax.psum((local_q, local_k, local_v), 'gy')  213 us
    ppermute x2, waiting for transfers between devices, with_halo(): before = lax.ppermute(last, axis, up)  37.3 us
    ppermute x2, waiting for transfers between devices, with_halo(): after = lax.ppermute(initial, axis, down)  31.8 us
    ppermute x4, waiting for transfers between devices, passed_along(): lax.ppermute(value, axis, [(source, source + steps) for source in range(i...  21.3 us
    dot_general x2, matrix products, one_slot(): jnp.einsum('hqk,qhd->khd', dscore, qh, preferred_element_type=jnp.float32)  17.7 us
    dot_general x2, matrix products, one_slot(): jnp.einsum('hqk,khd->qhd', dscore, kk, preferred_element_type=jnp.float32)  17.1 us
    ppermute x4, starting transfers between devices, passed_along(): lax.ppermute(value, axis, [(source, source + steps) for source in range(i...  14.2 us
  transfers between devices with their start and end apart: 9, of which 6 were waited for; matrix products, arithmetic and copies ran while one was open for 1% of the time, Pallas kernels for 0%

profile of v1, /device:TPU:104, one launch (start us, length us, event | category | flops | bytes accessed | tf_op | source)
XLA Modules:
  0.0 689.0 jit_solution(1554229484138471070)
XLA Ops:
  11.5 3.1 collective-permute-start
  17.5 2.1 collective-permute-start.2
  20.6 3.7 collective-permute-start.3
  28.0 37.0 %collective-permute-done.2 = bf16[3,1,2,128,1024]{4,3,2,1,0:T(8,128)(2,1)} collective-permute-done((bf16[3,1,2,128,1024]{4,3,2,1,0:T(8,128)(2,1)}, bf16[3,1,2,128,1024]{4,3,2,1,0:T(8,128)(2,1)}, u32[]{:S(2)}, u32[]{:S(2)}) %collective-permute-start.2) | collective-permute-done | bytes 1572896 | tf_op jit(solution)/shard_map/ppermute | solution.py:16
  64.9 1.9 fusion.46
  66.8 31.8 %collective-permute-done.3 = bf16[3,1,2,128,1024]{4,3,2,1,0:T(8,128)(2,1)S(1)} collective-permute-done((bf16[3,1,2,128,1024]{4,3,2,1,0:T(8,128)(2,1)}, bf16[3,1,2,128,1024]{4,3,2,1,0:T(8,128)(2,1)S(1)}, u32[]{:S(2)}, u32[]{:S(2)}) %collective-permute-start.3) | collective-permute-done | bytes 1572896 | tf_op jit(solution)/shard_map/ppermute | solution.py:17
  99.5 3.8 gather_fusion
  103.3 81.1 %while.14 = (s32[]{:T(128)}, bf16[2,128,512]{2,1,0:T(8,128)(2,1)}, bf16[2,128,512]{2,1,0:T(8,128)(2,1)}, f32[2,4,128,1024]{3,2,1,0:T(8,128)}, pred[2,128]{1,0:T(...) while((s32[]{:T(128)}, bf16[2,128,512]{2,1,0:T(8,128)(2,1)}, ...), condition=%wide.region_4.5_spmd, body=%wide.region_0.4_spmd.sunk | while | flops 415043072 | bytes 50373096 | solution.py:66
  109.7 3.9 fusion.108
  113.6 2.8 fusion.110
  116.4 8.5 %fusion.109 = bf16[8,64,128]{2,1,0:T(8,128)(2,1)} fusion(bf16[512,8,64]{0,2,1:T(8,128)(2,1)} %bitcast.165, f32[8,128,512]{2,1,0:T(8,128)S(1)} %fusion.107, f32[8,128,512]{2,1,0:T(8,128)} %get-tuple-element.185, f32[8,128]{1,0:T(8,128)S(1)} %copy-done.16), kind=kOutput, calls=%fused_computation.15.clone.1 | convolution fusion | flops 70845952 | bytes 4853760 | tf_op jit(solution)/shard_map/while/body/eval_jaxpr/hqk,khd->qhd/dot_general | solution.py:50
  124.9 8.8 %fusion.111 = f32[512,8,64]{0,2,1:T(8,128)} fusion(bf16[128,8,64]{0,2,1:T(8,128)(2,1)S(1)} %bitcast.180, f32[8,128,512]{2,1,0:T(8,128)S(1)} %fusion.107, f32[8,128,512]{2,1,0:T(8,128)} %get-tuple-element.185, f32[8,128]{1,0:T(8,128)S(1)} %copy-done.16), kind=kOutput, calls=%fused_computation.12.clone.1 | convolution fusion | flops 70780416 | bytes 5378048 | tf_op jit(solution)/shard_map/while/body/eval_jaxpr/hqk,qhd->khd/dot_general | solution.py:52
  133.8 2.0 convolution_bitcast_fusion.5
  137.7 1.8 maximum_bitcast_fusion.2
  139.5 2.0 copy.65
  150.3 3.9 fusion.108
  154.1 2.8 fusion.110
  156.9 8.5 %fusion.109 = bf16[8,64,128]{2,1,0:T(8,128)(2,1)} fusion(bf16[512,8,64]{0,2,1:T(8,128)(2,1)} %bitcast.165, f32[8,128,512]{2,1,0:T(8,128)S(1)} %fusion.107, f32[8,128,512]{2,1,0:T(8,128)} %get-tuple-element.185, f32[8,128]{1,0:T(8,128)S(1)} %copy-done.16), kind=kOutput, calls=%fused_computation.15.clone.1 | convolution fusion | flops 70845952 | bytes 4853760 | tf_op jit(solution)/shard_map/while/body/eval_jaxpr/hqk,khd->qhd/dot_general | solution.py:50
  165.5 8.8 %fusion.111 = f32[512,8,64]{0,2,1:T(8,128)} fusion(bf16[128,8,64]{0,2,1:T(8,128)(2,1)S(1)} %bitcast.180, f32[8,128,512]{2,1,0:T(8,128)S(1)} %fusion.107, f32[8,128,512]{2,1,0:T(8,128)} %get-tuple-element.185, f32[8,128]{1,0:T(8,128)S(1)} %copy-done.16), kind=kOutput, calls=%fused_computation.12.clone.1 | convolution fusion | flops 70780416 | bytes 5378048 | tf_op jit(solution)/shard_map/while/body/eval_jaxpr/hqk,qhd->khd/dot_general | solution.py:52
  174.3 2.0 convolution_bitcast_fusion.5
  178.2 1.8 maximum_bitcast_fusion.2
  180.0 2.0 copy.65
  184.5 4.6 copy.40
  189.1 3.6 convolution_convert_fusion
  192.7 1.9 fusion.50
  195.0 4.4 collective-permute-start.5
  199.5 4.0 collective-permute-start.6
  203.5 4.5 collective-permute-start.7
  210.7 8.2 %collective-permute-done.6 = bf16[2,128,1024]{2,1,0:T(8,128)(2,1)S(1)} collective-permute-done((bf16[2,128,1024]{2,1,0:T(8,128)(2,1)S(1)}, bf16[2,128,1024]{2,1,0:T(8,128)(2,1)S(1)}, u32[]{:S(2)}, u32[]{:S(2)}) %collective-permute-start.6) | collective-permute-done | bytes 524320 | tf_op jit(solution)/shard_map/ppermute | solution.py:25
  218.9 13.1 %collective-permute-done.7 = bf16[2,128,1024]{2,1,0:T(8,128)(2,1)S(1)} collective-permute-done((bf16[2,128,1024]{2,1,0:T(8,128)(2,1)S(1)}, bf16[2,128,1024]{2,1,0:T(8,128)(2,1)S(1)}, u32[]{:S(2)}, u32[]{:S(2)}) %collective-permute-start.7) | collective-permute-done | bytes 524320 | tf_op jit(solution)/shard_map/ppermute | solution.py:25
  237.8 212.7 %all-reduce.5.cloned.1.call-done = (f32[512,512]{0,1:T(8,128)}, f32[512,512]{0,1:T(8,128)}, f32[512,512]{0,1:T(8,128)}) async-done(((f32[512,512]{0,1:T(8,128)}, f32[512,512]{0,1:T(8,128)}, f32[512,512]{0,1:T(8,128)}), (f32[512,512]{0,1:T(8,128)}, f32[512,512]{0,1:T(8,128)}, f32[512,512]{0,1:T(8,128)})) %all-reduce.5.cloned.1.call-update) | async-done | bytes 3145744 | tf_op jit(solution)/shard_map/psum | solution.py:125
  450.4 228.7 %all-reduce.6 = (bf16[512,512]{0,1:T(8,128)(2,1)S(1)}, bf16[512,512]{0,1:T(8,128)(2,1)S(1)}, bf16[512,512]{0,1:T(8,128)(2,1)S(1)}) all-reduce(f32[512,512]{0,1:T(8,128)} %get-tuple-element.106, f32[512,512]{0,1:T(8,128)} %get-tuple-element.107, f32[512,512]{0,1:T(8,128)} %get-tuple-element.108), channel_id=1, replica_groups=mesh['gx'=32,'gy'=16] {'gx'}, use_global_device_ids=true, to_apply=%region_6.7 | all-reduce | flops 786432 | bytes 4718592 | tf_op jit(solution)/shard_map/psum | solution.py:125
  (130 shorter events, 45.1 us)
Async XLA Ops:
  7.2 18.1 %copy-start = (bf16[512,512]{1,0:T(8,128)(2,1)S(1)}, bf16[512,512]{1,0:T(8,128)(2,1)}, u32[]{:S(2)}) copy-start(bf16[512,512]{1,0:T(8,128)(2,1)} %param.12) | copy-start | bytes 1572868
  7.2 8.1 %copy-start.13 = (s32[1,1,2]{2,1,0:T(1,128)S(1)}, s32[1,1,2]{2,1,0:T(1,128)}, u32[]{:S(2)}) copy-start(s32[1,1,2]{2,1,0:T(1,128)} %param.17) | copy-start | bytes 28
  7.2 8.2 %copy-start.11 = (s32[1,1,2,3]{3,2,1,0:T(2,128)S(1)}, s32[1,1,2,3]{3,2,1,0:T(2,128)}, u32[]{:S(2)}) copy-start(s32[1,1,2,3]{3,2,1,0:T(2,128)} %param.18) | copy-start | bytes 76
  7.2 8.3 %copy-start.12 = (s32[1,1,2,3]{3,2,1,0:T(2,128)S(1)}, s32[1,1,2,3]{3,2,1,0:T(2,128)}, u32[]{:S(2)}) copy-start(s32[1,1,2,3]{3,2,1,0:T(2,128)} %param.19) | copy-start | bytes 76
  7.2 443.2 %all-reduce.5.cloned.1.call-start = ((), (), s32[]{:S(2)}) async-start(), calls=%async_computation | async-start | bytes 6291456 | tf_op jit(solution)/shard_map/psum | solution.py:125
  10.2 9.5 %copy-start.10 = (bf16[1,1,2,128,512]{4,3,2,1,0:T(8,128)(2,1)S(1)}, bf16[1,1,2,128,512]{4,3,2,1,0:T(8,128)(2,1)}, u32[]{:S(2)}) copy-start(bf16[1,1,2,128,512]{4,3,2,1,0:T(8,128)(2,1)} %param.15) | copy-start | bytes 786436
  10.2 5.5 collective-permute-start.1
  11.5 4.6 collective-permute-start
  15.7 9.6 %copy-start.1 = (bf16[1,1,2,128,512]{4,3,2,1,0:T(8,128)(2,1)S(1)}, bf16[1,1,2,128,512]{4,3,2,1,0:T(8,128)(2,1)}, u32[]{:S(2)}) copy-start(bf16[1,1,2,128,512]{4,3,2,1,0:T(8,128)(2,1)} %param.11) | copy-start | bytes 786436
  17.5 47.5 %collective-permute-start.2 = (bf16[3,1,2,128,1024]{4,3,2,1,0:T(8,128)(2,1)}, bf16[3,1,2,128,1024]{4,3,2,1,0:T(8,128)(2,1)}, u32[]{:S(2)}, u32[]{:S(2)}) collective-permute-start(bf16[3,1,2,128,1024]{4,3,2,1,0:T(8,128)(2,1)} %pad_maximum_fusion), channel_id=1, source_target_pairs={{0,1},{1,2},{2,3},{3,4},{4,5},{5,6},{6,7},{7,8},{8,9},{9,10},{10,1... | collective-permute-start | bytes 4718600 | tf_op jit(solution)/shard_map/ppermute | solution.py:16
  20.6 78.0 %collective-permute-start.3 = (bf16[3,1,2,128,1024]{4,3,2,1,0:T(8,128)(2,1)}, bf16[3,1,2,128,1024]{4,3,2,1,0:T(8,128)(2,1)S(1)}, u32[]{:S(2)}, u32[]{:S(2)}) collective-permute-start(bf16[3,1,2,128,1024]{4,3,2,1,0:T(8,128)(2,1)} %pad_maximum_fusion), channel_id=1, source_target_pairs={{1,0},{2,1},{3,2},{4,3},{5,4},{6,5},{7,6},{8,7},{9,8},{10,9},{11,1... | collective-permute-start | bytes 4718600 | tf_op jit(solution)/shard_map/ppermute | solution.py:17
  113.6 2.8 copy-start.16
  116.4 8.5 %copy-start.3 = (bf16[1,128,512]{1,2,0:T(8,128)(2,1)S(1)}, bf16[1,128,512]{1,2,0:T(8,128)(2,1)}, u32[]{:S(2)}) copy-start(bf16[1,128,512]{1,2,0:T(8,128)(2,1)} %copy.62) | copy-start | bytes 393220 | tf_op jit(solution)/shard_map/while
  139.5 2.0 copy-start.4
  139.5 2.1 copy-start.2
  139.5 2.3 copy-start.7
  142.4 1.5 copy-start.8
  142.4 1.5 copy-start.15
  154.1 2.8 copy-start.16
  156.9 8.5 %copy-start.3 = (bf16[1,128,512]{1,2,0:T(8,128)(2,1)S(1)}, bf16[1,128,512]{1,2,0:T(8,128)(2,1)}, u32[]{:S(2)}) copy-start(bf16[1,128,512]{1,2,0:T(8,128)(2,1)} %copy.62) | copy-start | bytes 393220 | tf_op jit(solution)/shard_map/while
  180.0 2.0 copy-start.4
  180.0 2.1 copy-start.2
  180.0 2.3 copy-start.7
  183.0 1.5 copy-start.8
  183.0 1.5 copy-start.15
  194.5 14.8 %copy-start.9 = (bf16[2,128,512]{2,1,0:T(8,128)(2,1)S(1)}, bf16[2,128,512]{2,1,0:T(8,128)(2,1)}, u32[]{:S(2)}) copy-start(bf16[2,128,512]{2,1,0:T(8,128)(2,1)} %get-tuple-element.55) | copy-start | bytes 786436
  195.0 15.6 %collective-permute-start.5 = (bf16[2,128,1024]{2,1,0:T(8,128)(2,1)S(1)}, bf16[2,128,1024]{2,1,0:T(8,128)(2,1)S(1)}, u32[]{:S(2)}, u32[]{:S(2)}) collective-permute-start(bf16[2,128,1024]{2,1,0:T(8,128)(2,1)S(1)} %bitcast.195), channel_id=1, source_target_pairs={{0,16},{16,32},{32,48},{48,64},{64,80},{80,96},{96,112},{112,128},... | collective-permute-start | bytes 1572872 | tf_op jit(solution)/shard_map/ppermute | solution.py:25
  199.5 19.4 %collective-permute-start.6 = (bf16[2,128,1024]{2,1,0:T(8,128)(2,1)S(1)}, bf16[2,128,1024]{2,1,0:T(8,128)(2,1)S(1)}, u32[]{:S(2)}, u32[]{:S(2)}) collective-permute-start(bf16[2,128,1024]{2,1,0:T(8,128)(2,1)S(1)} %bitcast.194), channel_id=1, source_target_pairs={{1,0},{2,1},{3,2},{4,3},{5,4},{6,5},{7,6},{8,7},{9,8},{10,9},{11,1... | collective-permute-start | bytes 1572872 | tf_op jit(solution)/shard_map/ppermute | solution.py:25
  203.5 28.5 %collective-permute-start.7 = (bf16[2,128,1024]{2,1,0:T(8,128)(2,1)S(1)}, bf16[2,128,1024]{2,1,0:T(8,128)(2,1)S(1)}, u32[]{:S(2)}, u32[]{:S(2)}) collective-permute-start(bf16[2,128,1024]{2,1,0:T(8,128)(2,1)S(1)} %bitcast.193), channel_id=1, source_target_pairs={{0,1},{1,2},{2,3},{3,4},{4,5},{5,6},{6,7},{7,8},{8,9},{9,10},{10,1... | collective-permute-start | bytes 1572872 | tf_op jit(solution)/shard_map/ppermute | solution.py:25
  208.0 24.0 %collective-permute-start.4 = (bf16[2,128,1024]{2,1,0:T(8,128)(2,1)S(1)}, bf16[2,128,1024]{2,1,0:T(8,128)(2,1)S(1)}, u32[]{:S(2)}, u32[]{:S(2)}) collective-permute-start(bf16[2,128,1024]{2,1,0:T(8,128)(2,1)S(1)} %bitcast.192), channel_id=1, source_target_pairs={{16,0},{32,16},{48,32},{64,48},{80,64},{96,80},{112,96},{128,112},... | collective-permute-start | bytes 1572872 | tf_op jit(solution)/shard_map/ppermute | solution.py:25
  235.3 1.0 copy-start.5
  235.4 1.4 copy-start.6
  (2 other events, 1.1 us)
Sparse Core Ops, SparseCore 0:
  235.5 214.8 all-reduce.4
